TPU v7x, 256 devices: a whole 4x4x8 slice. The times are simulated.
256 devices in a mesh: blk: 4 (over y_lo, core), grp: 64 (over y_hi, z, x).
Axes of the slice: x: 4, y: 4 (y_hi: 2, y_lo: 2; y = y_hi * 2 + y_lo), z: 8, core: 2. Of those that a mesh axis runs over, the one named last changes fastest.
Arguments:
- images: bfloat16 [12288, 1152], P('grp'), may hold values from -6 to 6
- texts: bfloat16 [12288, 1152], P(('blk', 'grp')), may hold values from -6 to 6
- log_temp: float32 [1], replicated, may hold values from -4 to -3
- bias: float32 [1], replicated, may hold values from -2 to 0
Outputs:
- loss: float32 [1], replicated
- grad_images: float32 [12288, 1152], P('grp')
- grad_texts: float32 [12288, 1152], P(('blk', 'grp'))
- grad_log_temp: float32 [1], replicated
- grad_bias: float32 [1], replicated
All inputs are finite; a program needn't handle non-finite values.
Results may differ from a plain program's by a relative error of at most 0.001.
The roundings to bfloat16 on the way count: a program that leaves them out, or rounds other values in their place, can miss the bound.
Values may be sent and summed in bfloat16 or wider, within the bound.
A program may use at most 64 MiB of HBM per device.

v0:
```python
import jax
import jax.numpy as jnp
from jax import lax
from jax.sharding import PartitionSpec as P


def local(images, texts, log_temp, bias):
    rows = images.shape[0]
    n_grp = lax.axis_size("grp")
    blk_id = lax.axis_index("blk")
    grp_id = lax.axis_index("grp")
    scale = jnp.exp(log_temp[0])
    shift_b = bias[0]
    quarter_txt = lax.all_gather(texts, "grp", axis=0, tiled=True)
    width = quarter_txt.shape[0]
    logits = scale * jnp.dot(images, quarter_txt.T, preferred_element_type=jnp.float32) + shift_b
    row_ids = grp_id * rows + jnp.arange(rows, dtype=jnp.int32)
    col_ids = blk_id * width + jnp.arange(width, dtype=jnp.int32)
    sign = jnp.where(row_ids[:, None] == col_ids[None, :], 1.0, -1.0).astype(jnp.float32)
    term = jax.nn.log_sigmoid(sign * logits)
    dlogit = -sign * jax.nn.sigmoid(-sign * logits)
    coef = (scale * dlogit).astype(jnp.bfloat16)
    loss_sum = -jnp.sum(term)
    temp_sum = jnp.sum(dlogit * (logits - shift_b))
    bias_sum = jnp.sum(dlogit)
    grad_part = jnp.dot(coef, quarter_txt, preferred_element_type=jnp.float32)
    partial_value = jnp.dot(coef.T, images, preferred_element_type=jnp.float32)
    grad_txt = lax.psum_scatter(partial_value, "grp", scatter_dimension=0, tiled=True)
    grad_img = lax.psum(grad_part, "blk")
    loss_all, temp_all, bias_all = lax.psum((loss_sum, temp_sum, bias_sum), ("blk", "grp"))
    total = jnp.float32(rows * n_grp)
    count = total * total
    return (
        jnp.reshape(loss_all / count, (1,)),
        grad_img,
        grad_txt,
        jnp.reshape(temp_all / count, (1,)),
        jnp.reshape(bias_all / count, (1,)),
    )


def solution(mesh):
    return jax.shard_map(
        local,
        mesh=mesh,
        in_specs=(P("grp", None), P(("blk", "grp"), None), P(), P()),
        out_specs=(P(), P("grp", None), P(("blk", "grp"), None), P(), P()),
        check_vma=False,
    )
```

profile of v0, /device:TPU:1, one launch (start us, length us, event | category | flops | bytes accessed | tf_op | source)
XLA Modules:
  0.0 1073.3 jit_solution(16261310251249761138)
XLA Ops:
  7.2 0.0 copy-start
  7.2 0.0 all-gather.2.cloned.1.call-start
  7.2 0.7 all-gather.2.cloned.1.call-update
  7.9 0.0 all-reduce.3.cloned.1.call-start
  9.3 144.2 %all-gather.2.cloned.1.call-done = bf16[3072,1152]{1,0:T(8,128)(2,1)} async-done(((bf16[48,1152]{1,0:T(8,128)(2,1)}), bf16[3072,1152]{1,0:T(8,128)(2,1)}) %all-gather.2.cloned.1.call-update) | async-done | bytes 7077904 | tf_op jit(solution)/shard_map/all_gather | solution.py:14
  153.5 0.0 copy-done
  153.5 0.0 copy-start.1
  153.5 7.9 fusion.12
  161.4 0.0 copy-done.1
  161.4 3.0 fusion.10
  164.4 0.0 all-reduce.3.cloned.1.call-update
  164.4 0.0 reduce-scatter.2.cloned.1.call-start
  164.5 8.1 fusion.9
  172.6 0.0 reduce-scatter.2.cloned.1.call-update
  172.6 78.5 %all-reduce = (f32[]{:T(128)}, f32[]{:T(128)}, f32[]{:T(128)}) all-reduce(f32[]{:T(128)} %get-tuple-element.7, f32[]{:T(128)} %get-tuple-element.6, f32[]{:T(128)} %get-tuple-element.5), channel_id=1, replica_groups=mesh['blk'=4,'grp'=64] {'blk','grp'}, use_global_device_ids=true, to_apply=%region_1.2 | all-reduce | flops 3 | bytes 24 | tf_op jit(solution)/shard_map/psum | solution.py:30
  253.0 0.0 all-reduce.3.cloned.1.call-done
  253.0 808.2 %reduce-scatter.2.cloned.1.call-done = f32[48,1152]{1,0:T(8,128)} async-done(((f32[3072,1152]{1,0:T(8,128)}), f32[48,1152]{1,0:T(8,128)}) %reduce-scatter.2.cloned.1.call-update) | async-done | bytes 221200 | tf_op jit(solution)/shard_map/reduce_scatter | solution.py:28
  1061.3 2.1 copy.12
  (2 shorter events, 0.0 us)
Async XLA Ops:
  7.2 146.3 %copy-start = (bf16[192,1152]{1,0:T(8,128)(2,1)S(1)}, bf16[192,1152]{1,0:T(8,128)(2,1)}, u32[]{:S(2)}) copy-start(bf16[192,1152]{1,0:T(8,128)(2,1)} %param.4) | copy-start | bytes 1327108
  7.2 146.3 %all-gather.2.cloned.1.call-start = ((), (), s32[]{:S(2)}) async-start(), calls=%async_computation.1 | async-start | bytes 7188480 | tf_op jit(solution)/shard_map/all_gather | solution.py:14
  7.9 245.1 %all-reduce.3.cloned.1.call-start = ((), (), s32[]{:S(2)}) async-start(), calls=%async_computation.2 | async-start | bytes 1769472 | tf_op jit(solution)/shard_map/psum | solution.py:29
  153.5 7.9 copy-start.1
  164.4 896.8 %reduce-scatter.2.cloned.1.call-start = ((), (), s32[]{:S(2)}) async-start(), calls=%async_computation.3 | async-start | bytes 14376960 | tf_op jit(solution)/shard_map/reduce_scatter | solution.py:28
Sparse Core Ops, SparseCore 0:
  11.7 141.7 all-gather.1
  164.6 45.5 all-reduce.2
  216.7 844.5 reduce-scatter.1
where the time goes:
time: 1080 us; the launch traced here: 1070 us
  waiting for transfers between devices  953 us (88%)
  blocking collectives  78.5 us (7%)
  between operations  20.4 us (2%)
  matrix products  19 us (2%)
    reduce_scatter x1, waiting for transfers between devices, local(): lax.psum_scatter(partial_value, 'grp', scatter_dimension=0, tiled=True)  808 us
    all_gather x1, waiting for transfers between devices, local(): quarter_txt = lax.all_gather(texts, 'grp', axis=0, tiled=True)  144 us
    psum x1, blocking collectives, local(): lax.psum((loss_sum, temp_sum, bias_sum), ('blk', 'grp'))  78.5 us
  transfers between devices with their start and end apart: 3, of which 2 were waited for; matrix products, arithmetic and copies ran while one was open for 1% of the time, Pallas kernels for 0%

commit v1 on v0

v1 whole, which is shorter than its diff:
```python
import functools

import jax
import jax.numpy as jnp
from jax import lax
from jax.experimental import pallas as pl
from jax.experimental.pallas import tpu as pltpu
from jax.sharding import PartitionSpec as P

MESH = pl.DeviceIdType.MESH
F32 = jnp.float32
BF16 = jnp.bfloat16

ROWS = 48
D = 1152
NX, NY, NZ = 4, 4, 8
SIDE = 16 * ROWS
SUB = 16

GROUPS = ((4, 3, 5), (2, 6), (1, 7, 0))
LOW, HIGH = 2.0**-6, 2.0**6 - 2.0**-6


def text_row(rel, other):
    base = 0
    for group in GROUPS:
        if rel in group:
            return base + (other * len(group) + group.index(rel)) * ROWS
        base += 2 * len(group) * ROWS
    raise ValueError(rel)


def encode(value):
    rows = value.shape[0]
    magnitude = jnp.abs(value)
    tall = jnp.max(magnitude.reshape(rows // 8, 8, D), axis=0)
    top = tall[:, :128]
    for i in range(1, D // 128):
        top = jnp.maximum(top, tall[:, 128 * i : 128 * i + 128])
    top = jnp.maximum(top, 1e-30)
    gain = jnp.concatenate([HIGH / top] * (D // 128), axis=1)
    t = magnitude.reshape(rows // 8, 8, D) * gain[None] + LOW
    for _ in range(4):
        t = t * t
    t = t.reshape(rows, D)
    return jnp.where(value < 0, -t, t).astype(BF16), top


def decode(code, top):
    rows = code.shape[0]
    v = code.astype(F32)
    gain = jnp.concatenate([top * (1.0 / HIGH)] * (D // 128), axis=1)
    t = jnp.exp2(jnp.log2(jnp.abs(v)) * 0.0625) - LOW
    t = (t.reshape(rows // 8, 8, D) * gain[None]).reshape(rows, D)
    return jnp.where(v < 0, -t, t)


def kernel(img, txt, lt, bs, loss_o, gimg_o, gtxt_o, temp_o, bias_o,
           I, T, PM, L, GI, GT, RT, rid, cid,
           ac_s, am_s, ac_r, am_r, zc_s, zm_s, zc_r, zm_r,
           sc_s, sc_x, sc_y, sc_z, sc_c, acc, ss, rs, ls):
    blk, grp = lax.axis_index("blk"), lax.axis_index("grp")
    lo, c = lax.div(blk, 2), lax.rem(blk, 2)
    h, z, x = lax.div(grp, 32), lax.rem(lax.div(grp, 4), 8), lax.rem(grp, 4)
    y = 2 * h + lo
    s = 1 - 2 * c

    def dev(x, y, z, c):
        return (lax.rem(y, 2) * 2 + c, lax.div(y, 2) * 32 + z * 4 + x)

    def at_x(d):
        return dev(lax.rem(x + d, 4), y, z, c)

    def at_y(d):
        return dev(x, lax.rem(y + d, 4), z, c)

    def at_z(d):
        return dev(x, y, lax.rem(z + s * d + 8, 8), c)

    def at_a(d):
        return dev(lax.rem(x + d * (1 - c), 4), lax.rem(y + d * c, 4), z, c)

    def at_b(d):
        return dev(lax.rem(x + d * c, 4), lax.rem(y + d * (1 - c), 4), z, c)

    at_core = dev(x, y, z, 1 - c)
    dyt, dyf = 1 + 2 * lo, 3 - 2 * lo

    barrier = pltpu.get_barrier_semaphore()
    peers = [at_x(1), at_x(2), at_x(3), at_y(1), at_y(2), at_y(3)] + [at_z(d) for d in range(1, 8)] + [at_core]
    for peer in peers:
        pl.semaphore_signal(barrier, inc=1, device_id=peer, device_id_type=MESH)

    def slot(dx, dy):
        return (dx * (1 + 3 * c) + dy * (4 - 3 * c)) * ROWS

    def rows_at(start, n, unit=ROWS):
        return pl.ds(pl.multiple_of(start, unit), n)

    mine = []
    for k, (dy, q) in enumerate(((0, lo), (dyt, 1 - lo))):
        mine.append(pltpu.make_async_copy(
            img.at[rows_at((q * 2 + c) * ROWS, ROWS)], I.at[rows_at(slot(0, dy), ROWS)], ls.at[k]))
    mine.append(pltpu.make_async_copy(txt, T.at[pl.ds(text_row(0, 0), ROWS)], ls.at[2]))
    for copy in mine:
        copy.start()

    for dy in range(4):
        for dx in range(4):
            x2, y2 = lax.rem(x + dx, 4), lax.rem(y + dy, 4)
            first = (lax.div(y2, 2) * 32 + z * 4 + x2) * 192 + (lax.rem(y2, 2) * 2 + c) * ROWS
            rid[rows_at(slot(dx, dy), ROWS), :] = first + lax.broadcasted_iota(jnp.int32, (ROWS, 128), 0)
    lane = lax.broadcasted_iota(jnp.int32, (8, SIDE), 1)
    ids = jnp.zeros((8, SIDE), jnp.int32)
    for rel in range(8):
        for other in range(2):
            z2 = lax.rem(z + (s if other == 0 else -s) * rel + 8, 8)
            c2 = c if other == 0 else 1 - c
            row = text_row(rel, other)
            first = (lo * 2 + c2) * 3072 + (h * 32 + z2 * 4 + x) * ROWS - row
            ids = jnp.where((lane >= row) & (lane < row + ROWS), lane + first, ids)
    cid[...] = ids
    acc[...] = jnp.zeros_like(acc)
    scale = jnp.exp(jnp.full((1, 128), lt[0], F32))
    shift = bs[0]

    pl.semaphore_wait(barrier, len(peers))

    sent = []
    count = [0]

    def send(src, dst, device):
        k = count[0]
        count[0] += 1
        copy = pltpu.make_async_remote_copy(
            src_ref=src, dst_ref=dst, send_sem=ss.at[k], recv_sem=rs.at[k], device_id=device, device_id_type=MESH)
        copy.start()
        sent.append(copy)
        return copy

    def send_piece(src, src_row, dst, dst_row, device, subs=3):
        n = ROWS // subs
        return [send(src.at[rows_at(src_row + i * n, n, n)], dst.at[rows_at(dst_row + i * n, n, n)], device)
                for i in range(subs)]

    def wait(copies):
        for copy in copies:
            copy.wait_recv()

    own_row, twin_row = (lo * 2 + c) * ROWS, ((1 - lo) * 2 + c) * ROWS
    t_p = {0: send_piece(txt, 0, T, text_row(7, 0), at_z(1))}
    t_m = {0: send_piece(txt, 0, T, text_row(1, 0), at_z(7))}
    xp0 = send_piece(img, own_row, I, slot(3, 0), at_x(1))
    xm1 = send_piece(img, twin_row, I, slot(1, dyt), at_x(3))
    yf0 = send_piece(img, own_row, I, slot(0, dyt), at_y(dyf))
    xp1 = send_piece(img, twin_row, I, slot(3, dyt), at_x(1))
    xm0 = send_piece(img, own_row, I, slot(1, 0), at_x(3))
    t_c = {0: send_piece(txt, 0, T, text_row(0, 1), at_core, 1)}

    xpf, xmf, y1, y2, y3, w0, w1, w2, w3 = [], [], [], [], [], [], [], [], []
    dxs, dxi = 1 + 2 * lo, 3 - 2 * lo

    def forward(copies, i, src, src_row, dst, dst_row, device, out):
        copies[i].wait_recv()
        out.append(send(src.at[rows_at(src_row + i * SUB, SUB, SUB)], dst.at[rows_at(dst_row + i * SUB, SUB, SUB)], device))

    def text_step(k):
        t_p[k], t_m[k] = [], []
        for i in range(3):
            forward(t_p[k - 1], i, T, text_row(8 - k, 0), T, text_row(7 - k, 0), at_z(1), t_p[k])
            if k < 3:
                forward(t_m[k - 1], i, T, text_row(k, 0), T, text_row(k + 1, 0), at_z(7), t_m[k])
        if k == 3:
            wait(t_m[2])
        t_c[8 - k] = send_piece(T, text_row(8 - k, 0), T, text_row(8 - k, 1), at_core, 1)
        t_c[k] = send_piece(T, text_row(k, 0), T, text_row(k, 1), at_core, 1)

    for i in range(3):
        forward(xp0, i, I, slot(3, 0), I, slot(2, 0), at_x(1), xpf)
        forward(xm1, i, I, slot(1, dyt), I, slot(2, dyt), at_x(3), xmf)
        forward(yf0, i, I, slot(0, dyf), I, slot(0, 2), at_y(dyt), w0)
    text_step(1)
    wait(xm0)
    for i in range(3):
        y1.append(send(I.at[rows_at(slot(dxs, 0) + i * SUB, SUB, SUB)],
                       I.at[rows_at(slot(dxs, dyt) + i * SUB, SUB, SUB)], at_y(dyf)))
    wait(xp1)
    for i in range(3):
        y2.append(send(I.at[rows_at(slot(dxs, dyt) + i * SUB, SUB, SUB)],
                       I.at[rows_at(slot(dxs, 2) + i * SUB, SUB, SUB)], at_y(dyf)))
    text_step(2)
    for i in range(3):
        forward(y1, i, I, slot(dxi, dyf), I, slot(dxi, 2), at_y(dyt), w1)
    for i in range(3):
        forward(xpf, i, I, slot(2, 0), I, slot(2, dyt), at_y(dyf), y3)
    text_step(3)
    for i in range(3):
        forward(y2, i, I, slot(dxi, 2), I, slot(dxi, dyt), at_y(dyt), w2)
    for i in range(3):
        forward(y3, i, I, slot(2, dyf), I, slot(2, 2), at_y(dyt), w3)
    wait(t_p[3])
    t_c[4] = send_piece(T, text_row(4, 0), T, text_row(4, 1), at_core, 1)
    for rel in range(8):
        wait(t_c[rel])
    for copy in mine:
        copy.wait()
    wait(xmf)
    for copies in (w0, w1, w2, w3):
        wait(copies)

    def pair(g):
        base = g * (4 * ROWS)
        L[...] = lax.dot_general(I[rows_at(base, 4 * ROWS), :], T[...], (((1,), (1,)), ((), ())),
                                 preferred_element_type=F32)

        def chunk(i, carry):
            r = pl.multiple_of(i * 16, 16)
            rg = pl.multiple_of(base + i * 16, 16)
            rows = rid[pl.ds(rg, 16), :]
            sums = list(carry)
            for j in range(0, SIDE, 384):
                dot = L[pl.ds(r, 16), j : j + 384] * jnp.concatenate([scale] * 3, axis=1)
                same = jnp.concatenate([rows] * 3, axis=1) == jnp.concatenate([cid[:, j : j + 384]] * 2, axis=0)
                logit = dot + shift
                signed = jnp.where(same, logit, -logit)
                e = jnp.exp(-jnp.abs(signed))
                inv = 1.0 / (1.0 + e)
                term = jnp.minimum(signed, 0.0) - jnp.log1p(e)
                d = jnp.where(signed >= 0, e, 1.0) * inv
                d = jnp.where(same, -d, d)
                PM[pl.ds(rg, 16), j : j + 384] = (d * jnp.concatenate([scale] * 3, axis=1)).astype(BF16)
                for n, v in enumerate((term, d * dot, d)):
                    for q in range(3):
                        w = v[:, 128 * q : 128 * q + 128]
                        sums[n] = sums[n] + (w[:8] + w[8:])
            return tuple(sums)

        zero = jnp.zeros((8, 128), F32)
        sums = lax.fori_loop(0, 12, chunk, (zero, zero, zero))
        for n in range(3):
            acc[8 * n : 8 * n + 8, :] += sums[n]
        GI[rows_at(base, 4 * ROWS), :] = jnp.dot(PM[rows_at(base, 4 * ROWS), :], T[...], preferred_element_type=F32)

    def send_code(k, row, device, dst=None):
        code, top = encode(GI[rows_at(row, ROWS), :])
        ac_s[k] = code
        am_s[k] = top
        dst = k if dst is None else dst
        return [send(ac_s.at[k], ac_r.at[dst], device), send(am_s.at[k], am_r.at[dst], device)]

    def got(k):
        return decode(ac_r[k], am_r[k])

    g1 = (1 + 2 * lo) * (1 - c) + c
    order = (0, g1, 4 - g1, 2)
    a2, am, ap, bb = {}, {}, {}, {}

    def first_sends(i):
        base = order[i] * (4 * ROWS)
        d = 1 if i % 2 == 0 else 3
        a2[i] = send_code(3 * i, base + 2 * ROWS, at_a(d))
        am[i] = send_code(3 * i + 1, base + (4 - d) * ROWS, at_a(4 - d))

    def add_on(i):
        base = order[i] * (4 * ROWS)
        d = 1 if i % 2 == 0 else 3
        wait(a2[i])
        GI[rows_at(base + d * ROWS, ROWS), :] += got(3 * i)
        ap[i] = send_code(3 * i + 2, base + d * ROWS, at_a(d))

    def close(i):
        base = order[i] * (4 * ROWS)
        wait(am[i])
        wait(ap[i])
        GI[rows_at(base, ROWS), :] += got(3 * i + 1) + got(3 * i + 2)
        if i == 0:
            return
        code, top = encode(GI[rows_at(base, ROWS), :])
        ac_s[11 + i] = code
        am_s[11 + i] = top
        g = order[i]
        if i == 3:
            bb[3] = [send(ac_s.at[14], ac_r.at[14], at_b(2)), send(am_s.at[14], am_r.at[14], at_b(2))]
        else:
            k = 12 + lax.div(g, 2)
            base_k = count[0] if i == 1 else bb["k"]
            if i == 1:
                bb["k"] = base_k
                count[0] += 4
            copies = []
            for n, (src, dst) in enumerate(((ac_s, ac_r), (am_s, am_r))):
                sem = base_k + 2 * n + lax.div(g, 2)
                copy = pltpu.make_async_remote_copy(
                    src_ref=src.at[11 + i], dst_ref=dst.at[k], send_sem=ss.at[sem], recv_sem=rs.at[sem],
                    device_id=at_b(g), device_id_type=MESH)
                copy.start()
                sent.append(copy)
                copies.append(copy)
            bb[i] = copies

    cores = {}

    def text_grads(g):
        n = len(GROUPS[g]) * ROWS
        base = text_row(GROUPS[g][0], 0)
        GT[pl.ds(base, 2 * n), :] = lax.dot_general(PM[:, base : base + 2 * n], I[...], (((0,), (0,)), ((), ())),
                                                    preferred_element_type=F32)
        half = text_half(g)
        cores[g] = send(GT.at[pl.ds(base + n, n)], RT.at[pl.ds(half, n)], at_core)

    def text_half(g):
        return sum(len(GROUPS[i]) for i in range(g)) * ROWS

    def text_join(g):
        n = len(GROUPS[g]) * ROWS
        base = text_row(GROUPS[g][0], 0)
        cores[g].wait_recv()
        GT[pl.ds(base, n), :] += RT[pl.ds(text_half(g), n), :]

    zs = {}

    def z_send(chain, step, i, rel, incoming):
        row = text_row(rel, 0) + i * SUB
        value = GT[row : row + SUB, :]
        k = ((0 if chain == "p" else 4) + step) * 3 + i
        if incoming:
            wait(zs[chain, step - 1, i])
            value = value + decode(zc_r[k - 3], zm_r[k - 3])
        code, top = encode(value)
        zc_s[k] = code
        zm_s[k] = top
        device = at_z(1) if chain == "p" else at_z(7)
        zs[chain, step, i] = [send(zc_s.at[k], zc_r.at[k], device), send(zm_s.at[k], zm_r.at[k], device)]

    for i in range(4):
        pair(order[i])
        first_sends(i)
        if i:
            add_on(i - 1)
    sc_s[0] = acc[...]
    sc = {"c": send(sc_s.at[0], sc_c, at_core)}
    text_grads(0)
    add_on(3)
    text_join(0)
    for i in range(3):
        z_send("p", 0, i, 4, False)
        z_send("m", 0, i, 5, False)
    text_grads(1)
    close(0)
    close(1)
    sc["c"].wait_recv()
    sc_s[1] = sc_s[0] + sc_c[...]
    sc_x[x] = sc_s[1]
    sc["x"] = [send(sc_s.at[1], sc_x.at[x], at_x(d)) for d in (1, 2, 3)]
    for i in range(3):
        z_send("p", 1, i, 3, True)
    text_join(1)
    for i in range(3):
        z_send("m", 1, i, 6, True)
    text_grads(2)
    close(2)
    wait(sc["x"])
    sc_s[2] = (sc_x[0] + sc_x[1]) + (sc_x[2] + sc_x[3])
    sc_y[y] = sc_s[2]
    sc["y"] = [send(sc_s.at[2], sc_y.at[y], at_y(d)) for d in (1, 2, 3)]
    for i in range(3):
        z_send("p", 2, i, 2, True)
    text_join(2)
    for i in range(3):
        z_send("m", 2, i, 7, True)
    close(3)
    wait(sc["y"])
    sc_s[3] = (sc_y[0] + sc_y[1]) + (sc_y[2] + sc_y[3])
    sc_z[z] = sc_s[3]
    sc["z"] = [send(sc_s.at[3], sc_z.at[z], at_z(d)) for d in range(1, 8)]
    for i in range(3):
        z_send("p", 3, i, 1, True)
    for i in (1, 2, 3):
        wait(bb[i])
    GI[0:ROWS, :] += got(12) + got(13) + got(14)
    code, top = encode(GI[0:ROWS, :])
    ac_s[15] = code
    am_s[15] = top
    twin = [send(ac_s.at[15], ac_r.at[15], at_y(dyt)), send(am_s.at[15], am_r.at[15], at_y(dyt))]
    side = [send(ac_s.at[15], ac_r.at[16], at_core), send(am_s.at[15], am_r.at[16], at_core)]
    gimg_o[rows_at(own_row, ROWS), :] = decode(code, top)
    for i in range(3):
        row = text_row(0, 0) + i * SUB
        wait(zs["p", 3, i])
        wait(zs["m", 2, i])
        kp, km = 3 * 3 + i, 6 * 3 + i
        gtxt_o[i * SUB : i * SUB + SUB, :] = (GT[row : row + SUB, :] + decode(zc_r[kp], zm_r[kp])
                                              + decode(zc_r[km], zm_r[km]))
    wait(sc["z"])
    total = sc_z[0]
    for i in range(1, 8):
        total = total + sc_z[i]
    pairs = 1.0 / (256.0 * ROWS * 256.0 * ROWS)
    loss_o[0] = -jnp.sum(total[0:8]) * pairs
    temp_o[0] = jnp.sum(total[8:16]) * pairs
    bias_o[0] = jnp.sum(total[16:24]) * pairs
    wait(twin)
    pair_side = [send(ac_r.at[15], ac_r.at[17], at_core), send(am_r.at[15], am_r.at[17], at_core)]
    gimg_o[rows_at(twin_row, ROWS), :] = got(15)
    wait(side)
    gimg_o[rows_at((lo * 2 + 1 - c) * ROWS, ROWS), :] = got(16)
    wait(pair_side)
    gimg_o[rows_at(((1 - lo) * 2 + 1 - c) * ROWS, ROWS), :] = got(17)
    for copy in sent:
        copy.wait_send()


def local(images, texts, log_temp, bias):
    sems = 220
    vmem = pl.BlockSpec(memory_space=pltpu.VMEM)
    smem = pl.BlockSpec(memory_space=pltpu.SMEM)
    hbm = pl.BlockSpec(memory_space=pl.ANY)
    scalar = jax.ShapeDtypeStruct((1,), F32)
    V = pltpu.VMEM
    return pl.pallas_call(
        kernel,
        out_shape=(scalar, jax.ShapeDtypeStruct((4 * ROWS, D), F32), jax.ShapeDtypeStruct((ROWS, D), F32), scalar, scalar),
        in_specs=[hbm, hbm, smem, smem],
        out_specs=(smem, vmem, vmem, smem, smem),
        scratch_shapes=[
            V((SIDE, D), BF16), V((SIDE, D), BF16), V((SIDE, SIDE), BF16), V((4 * ROWS, SIDE), F32),
            V((SIDE, D), F32), V((SIDE, D), F32), V((SIDE // 2, D), F32),
            V((SIDE, 128), jnp.int32), V((8, SIDE), jnp.int32),
            V((16, ROWS, D), BF16), V((16, 8, 128), F32), V((18, ROWS, D), BF16), V((18, 8, 128), F32),
            V((21, SUB, D), BF16), V((21, 8, 128), F32), V((21, SUB, D), BF16), V((21, 8, 128), F32),
            V((4, 24, 128), F32), V((4, 24, 128), F32), V((4, 24, 128), F32), V((8, 24, 128), F32),
            V((24, 128), F32), V((24, 128), F32),
            pltpu.SemaphoreType.DMA((sems,)), pltpu.SemaphoreType.DMA((sems,)), pltpu.SemaphoreType.DMA((3,)),
        ],
        compiler_params=pltpu.CompilerParams(collective_id=0, has_side_effects=True, vmem_limit_bytes=48 << 20),
        name="pairs",
    )(images, texts, log_temp, bias)


def solution(mesh):
    return jax.shard_map(
        local,
        mesh=mesh,
        in_specs=(P("grp", None), P(("blk", "grp"), None), P(), P()),
        out_specs=(P(), P("grp", None), P(("blk", "grp"), None), P(), P()),
        check_vma=False,
    )
```

time: 1080 us -> 80.3 us (0.07)
  waiting for transfers between devices: 953 us -> 0 us
  blocking collectives: 78.5 us -> 0 us
  Pallas kernels: 0 us -> 69.4 us
  matrix products: 19 us -> 0 us
  between operations: 20.4 us -> 7.18 us
    reduce_scatter x1 -> x0, waiting for transfers between devices: 808 us -> none  [local(): lax.psum_scatter(partial_value, 'grp', scatter_dimension=0, tiled=True)]
    all_gather x1 -> x0, waiting for transfers between devices: 144 us -> none  [local(): quarter_txt = lax.all_gather(texts, 'grp', axis=0, tiled=True)]
    psum x1 -> x0, blocking collectives: 78.5 us -> none  [local(): lax.psum((loss_sum, temp_sum, bias_sum), ('blk', 'grp'))]
    pallas_call x0 -> x1, Pallas kernels: none -> 69.4 us  [local(): pl.pallas_call(kernel, out_shape=(scalar, jax.ShapeDtypeStruct((4 * ROWS,...]
    dot_general x3 -> x0, matrix products: 19 us -> none  [the longest x1 8.06 us: local(): partial_value = jnp.dot(coef.T, images, preferred_element_type=jnp.float32)]
  transfers between devices with their start and end apart: 3 -> 0, of which waited for: 2 -> 0; matrix products, arithmetic and copies ran while one was open for 1% -> 0% of each run, Pallas kernels for 0% -> 0%
where the time goes in v1:
time: 80.3 us; the launch traced here: 80.1 us
  Pallas kernels  69.4 us (86%)
  between operations  7.18 us (9%)
  local copies, waits for them, and re-layouts  3.5 us (4%)
    pallas_call x1, Pallas kernels, local(): pl.pallas_call(kernel, out_shape=(scalar, jax.ShapeDtypeStruct((4 * ROWS,...  69.4 us
    unnamed x6, local copies, waits for them, and re-layouts  3.5 us

profile of v1, /device:TPU:1, one launch (start us, length us, event | category | flops | bytes accessed | tf_op | source)
XLA Modules:
  0.0 80.1 jit_solution(7685532288197681117)
XLA Ops:
  1.9 0.0 copy-start
  1.9 1.0 %copy-done = bf16[192,1152]{1,0:T(8,128)(2,1)S(1)} copy-done((bf16[192,1152]{1,0:T(8,128)(2,1)S(1)}, bf16[192,1152]{1,0:T(8,128)(2,1)}, u32[]{:S(2)}) %copy-start) | copy-done | bytes 442392
  2.9 0.0 copy-start.1
  2.9 0.9 %copy-done.1 = bf16[48,1152]{1,0:T(8,128)(2,1)S(1)} copy-done((bf16[48,1152]{1,0:T(8,128)(2,1)S(1)}, bf16[48,1152]{1,0:T(8,128)(2,1)}, u32[]{:S(2)}) %copy-start.1) | copy-done | bytes 110616
  3.8 69.4 %pairs.1 = (f32[1]{0:T(128)}, f32[192,1152]{1,0:T(8,128)S(1)}, f32[48,1152]{1,0:T(8,128)S(1)}, f32[1]{0:T(128)}, f32[1]{0:T(128)}) custom-call(bf16[192,1152]{1,0:T(8,128)(2,1)S(1)} %copy-done, bf16[48,1152]{1,0:T(8,128)(2,1)S(1)} %copy-done.1, f32[1]{0:T(128)S(6)} %copy.14.lt, f32[1]{0:T(128)S(6)} %copy.15.bs), custom_call_target="tpu_custom_call" | custom-call | tf_op jit(solution)/shard_map/pairs/pallas_call | solution.py:420
  73.9 0.9 %copy.17 = f32[192,1152]{1,0:T(8,128)} copy(f32[192,1152]{1,0:T(8,128)S(1)} %get-tuple-element.11) | data formatting | bytes 1769472
  74.8 0.7 copy.18
Async XLA Ops:
  1.9 1.0 %copy-start = (bf16[192,1152]{1,0:T(8,128)(2,1)S(1)}, bf16[192,1152]{1,0:T(8,128)(2,1)}, u32[]{:S(2)}) copy-start(bf16[192,1152]{1,0:T(8,128)(2,1)} %img.1) | copy-start | bytes 1327108
  2.9 0.9 %copy-start.1 = (bf16[48,1152]{1,0:T(8,128)(2,1)S(1)}, bf16[48,1152]{1,0:T(8,128)(2,1)}, u32[]{:S(2)}) copy-start(bf16[48,1152]{1,0:T(8,128)(2,1)} %txt.1) | copy-start | bytes 331780

commit v2 on v0

v2 whole, which is shorter than its diff:
```python
import functools

import jax
import jax.numpy as jnp
from jax import lax
from jax.experimental import pallas as pl
from jax.experimental.pallas import tpu as pltpu
from jax.sharding import PartitionSpec as P

MESH = pl.DeviceIdType.MESH
F32 = jnp.float32
BF16 = jnp.bfloat16

ROWS = 48
D = 1152
NX, NY, NZ = 4, 4, 8
SIDE = 16 * ROWS
SUB = 16
HALF = SIDE // 2

GROUPS = ((4, 3, 5), (2, 6), (1, 7, 0))
LOW, HIGH = 2.0**-6, 2.0**6 - 2.0**-6


def text_row(rel, other):
    base = 0
    for group in GROUPS:
        if rel in group:
            return base + (other * len(group) + group.index(rel)) * ROWS
        base += 2 * len(group) * ROWS
    raise ValueError(rel)


def encode(value, message):
    tiles = [(r, j) for r in range(0, value.shape[0], 16) for j in range(0, D, 128)]
    top = jnp.full((16, 128), 1e-30, F32)
    for r, j in tiles:
        top = jnp.maximum(top, jnp.abs(value[r : r + 16, j : j + 128]))
    top = (top * 1.004).astype(BF16)
    gain = HIGH / top.astype(F32)
    for n, (r, j) in enumerate(tiles):
        v = value[r : r + 16, j : j + 128]
        t = jnp.abs(v) * gain + LOW
        for _ in range(4):
            t = t * t
        message[n] = jnp.where(v < 0, -t, t).astype(BF16)
    message[len(tiles)] = top


def decode(message, rows):
    count = rows // 16 * (D // 128)
    gain = message[count].astype(F32) * (1.0 / HIGH)
    out = []
    for n in range(count):
        v = message[n].astype(F32)
        t = (jnp.exp2(jnp.log2(jnp.abs(v)) * 0.0625) - LOW) * gain
        out.append(jnp.where(v < 0, -t, t))
    width = D // 128
    return jnp.concatenate(
        [jnp.concatenate(out[i : i + width], axis=1) for i in range(0, count, width)], axis=0)


def kernel(img, txt, lt, bs, loss_o, gimg_o, gtxt_o, temp_o, bias_o,
           I, T, PM, L, GI, GT, RT, rid, cid,
           img_s, img_r, txt_s, txt_r,
           sc_s, sc_x, sc_y, sc_z, sc_c, acc, ss, rs, ls):
    blk, grp = lax.axis_index("blk"), lax.axis_index("grp")
    lo, c = lax.div(blk, 2), lax.rem(blk, 2)
    h, z, x = lax.div(grp, 32), lax.rem(lax.div(grp, 4), 8), lax.rem(grp, 4)
    y = 2 * h + lo
    s = 1 - 2 * c

    def dev(x, y, z, c):
        return (lax.rem(y, 2) * 2 + c, lax.div(y, 2) * 32 + z * 4 + x)

    def at_x(d):
        return dev(lax.rem(x + d, 4), y, z, c)

    def at_y(d):
        return dev(x, lax.rem(y + d, 4), z, c)

    def at_z(d):
        return dev(x, y, lax.rem(z + s * d + 8, 8), c)

    def at_a(d):
        return dev(lax.rem(x + d * (1 - c), 4), lax.rem(y + d * c, 4), z, c)

    def at_b(d):
        return dev(lax.rem(x + d * c, 4), lax.rem(y + d * (1 - c), 4), z, c)

    at_core = dev(x, y, z, 1 - c)
    dyt, dyf = 1 + 2 * lo, 3 - 2 * lo

    barrier = pltpu.get_barrier_semaphore()
    peers = [at_x(1), at_x(2), at_x(3), at_y(1), at_y(2), at_y(3)] + [at_z(d) for d in range(1, 8)]
    peers += [at_core]
    for peer in peers:
        pl.semaphore_signal(barrier, inc=1, device_id=peer, device_id_type=MESH)

    def slot(dx, dy):
        return (dx * (1 + 3 * c) + dy * (4 - 3 * c)) * ROWS

    def rows_at(start, n, unit=ROWS):
        return pl.ds(pl.multiple_of(start, unit), n)

    mine = []
    for k, (dy, q) in enumerate(((0, lo), (dyt, 1 - lo))):
        mine.append(pltpu.make_async_copy(
            img.at[rows_at((q * 2 + c) * ROWS, ROWS)], I.at[rows_at(slot(0, dy), ROWS)], ls.at[k]))
    mine.append(pltpu.make_async_copy(txt, T.at[pl.ds(text_row(0, 0), ROWS)], ls.at[2]))
    for copy in mine:
        copy.start()

    for dy in range(4):
        for dx in range(4):
            x2, y2 = lax.rem(x + dx, 4), lax.rem(y + dy, 4)
            first = (lax.div(y2, 2) * 32 + z * 4 + x2) * 192 + (lax.rem(y2, 2) * 2 + c) * ROWS
            rid[rows_at(slot(dx, dy), ROWS), :] = first + lax.broadcasted_iota(jnp.int32, (ROWS, 128), 0)
    lane = lax.broadcasted_iota(jnp.int32, (8, SIDE), 1)
    ids = jnp.zeros((8, SIDE), jnp.int32)
    for rel in range(8):
        for other in range(2):
            z2 = lax.rem(z + (s if other == 0 else -s) * rel + 8, 8)
            c2 = c if other == 0 else 1 - c
            row = text_row(rel, other)
            first = (lo * 2 + c2) * 3072 + (h * 32 + z2 * 4 + x) * ROWS - row
            ids = jnp.where((lane >= row) & (lane < row + ROWS), lane + first, ids)
    cid[...] = ids
    acc[...] = jnp.zeros_like(acc)
    scale = jnp.exp(jnp.full((1, 128), lt[0], F32))
    shift = bs[0]

    pl.semaphore_wait(barrier, len(peers))

    sent = []
    count = [0]

    def send(src, dst, device, sem=None):
        k = count[0] if sem is None else sem
        if sem is None:
            count[0] += 1
        copy = pltpu.make_async_remote_copy(
            src_ref=src, dst_ref=dst, send_sem=ss.at[k], recv_sem=rs.at[k], device_id=device, device_id_type=MESH)
        copy.start()
        sent.append(copy)
        return copy

    def send_piece(src, src_row, dst, dst_row, device, subs=3):
        n = ROWS // subs
        return [send(src.at[rows_at(src_row + i * n, n, n)], dst.at[rows_at(dst_row + i * n, n, n)], device)
                for i in range(subs)]

    def wait(copies):
        for copy in copies:
            copy.wait_recv()

    own_row, twin_row = (lo * 2 + c) * ROWS, ((1 - lo) * 2 + c) * ROWS
    dxs, dxi = 1 + 2 * lo, 3 - 2 * lo

    def hop(src, src_row, dst, dst_row, i, device):
        return send(src.at[rows_at(src_row + i * SUB, SUB, SUB)], dst.at[rows_at(dst_row + i * SUB, SUB, SUB)], device)

    def text_hop(rel, into, i, distance):
        return hop(T, text_row(rel, 0), T, text_row(into, 0), i, at_z(distance))

    t7, t1, t6, t2, t5, t4, t3 = [], [], [], [], [], [], []
    xp0, xm1, xp1, xm0, yf0 = [], [], [], [], []
    for i in range(3):
        t7.append(hop(txt, 0, T, text_row(7, 0), i, at_z(1)))
        t1.append(hop(txt, 0, T, text_row(1, 0), i, at_z(7)))
        xp0.append(hop(img, own_row, I, slot(3, 0), i, at_x(1)))
        xm1.append(hop(img, twin_row, I, slot(1, dyt), i, at_x(3)))
        yf0.append(hop(img, own_row, I, slot(0, dyt), i, at_y(dyf)))
    for i in range(3):
        xp1.append(hop(img, twin_row, I, slot(3, dyt), i, at_x(1)))
        xm0.append(hop(img, own_row, I, slot(1, 0), i, at_x(3)))
    t_c = [send_piece(txt, 0, T, text_row(0, 1), at_core, 1)]

    xpf, xmf, y1, y2, w0, w1, w2, v1, v2 = [], [], [], [], [], [], [], [], []
    for i in range(3):
        t7[i].wait_recv()
        t6.append(text_hop(7, 6, i, 1))
        t1[i].wait_recv()
        t2.append(text_hop(1, 2, i, 7))
        xp0[i].wait_recv()
        xm1[i].wait_recv()
        y1.append(hop(I, slot(dxs, 1 - lo), I, slot(dxs, 2 + lo), i, at_y(dyf)))
        xpf.append(hop(I, slot(3, 0), I, slot(2, 0), i, at_x(1)))
        xmf.append(hop(I, slot(1, dyt), I, slot(2, dyt), i, at_x(3)))
        yf0[i].wait_recv()
        w0.append(hop(I, slot(0, dyf), I, slot(0, 2), i, at_y(dyt)))
    t_c.append(send_piece(T, text_row(7, 0), T, text_row(7, 1), at_core, 1))
    t_c.append(send_piece(T, text_row(1, 0), T, text_row(1, 1), at_core, 1))
    for i in range(3):
        xp1[i].wait_recv()
        xm0[i].wait_recv()
        y2.append(hop(I, slot(dxs, 3 * lo), I, slot(dxs, 1 + lo), i, at_y(dyf)))
    for i in range(3):
        y1[i].wait_recv()
        w1.append(hop(I, slot(dxi, 3 - lo), I, slot(dxi, 2 + lo), i, at_y(dyt)))
        v1.append(hop(I, slot(dxi, 3 - lo), I, slot(2, 3 - lo), i, at_x(dxs)))
        t6[i].wait_recv()
        t5.append(text_hop(6, 5, i, 1))
        t4.append(text_hop(6, 4, i, 2))
        t2[i].wait_recv()
        t3.append(text_hop(2, 3, i, 7))
    t_c.append(send_piece(T, text_row(6, 0), T, text_row(6, 1), at_core, 1))
    t_c.append(send_piece(T, text_row(2, 0), T, text_row(2, 1), at_core, 1))
    for i in range(3):
        y2[i].wait_recv()
        w2.append(hop(I, slot(dxi, 2 - lo), I, slot(dxi, 1 + lo), i, at_y(dyt)))
        v2.append(hop(I, slot(dxi, 2 - lo), I, slot(2, 2 - lo), i, at_x(dxs)))
    for i in range(3):
        for rel, copies in ((3, t3), (5, t5)):
            copies[i].wait_recv()
            t_c.append([hop(T, text_row(rel, 0), T, text_row(rel, 1), i, at_core)])
    for i in range(3):
        t4[i].wait_recv()
        t_c.append([hop(T, text_row(4, 0), T, text_row(4, 1), i, at_core)])
    for copies in t_c:
        wait(copies)
    for copy in mine:
        copy.wait()
    for copies in (xpf, xmf, w0, w1, w2, v1, v2):
        wait(copies)

    g1 = (1 + 2 * lo) * (1 - c) + c
    order = (2, g1, 4 - g1, 0)

    def pair(g, j):
        base = order[g] * (4 * ROWS)
        L[...] = lax.dot_general(I[rows_at(base, 4 * ROWS), :], T[j : j + HALF, :], (((1,), (1,)), ((), ())),
                                 preferred_element_type=F32)

        def chunk(i, carry):
            r = pl.multiple_of(i * 16, 16)
            rg = pl.multiple_of(base + i * 16, 16)
            rows = rid[pl.ds(rg, 16), :]
            sums = list(carry)
            dot = L[pl.ds(r, 16), :] * jnp.concatenate([scale] * 3, axis=1)
            same = jnp.concatenate([rows] * 3, axis=1) == jnp.concatenate([cid[:, j : j + HALF]] * 2, axis=0)
            logit = dot + shift
            signed = jnp.where(same, logit, -logit)
            e = jnp.exp(-jnp.abs(signed))
            inv = 1.0 / (1.0 + e)
            term = jnp.minimum(signed, 0.0) - jnp.log1p(e)
            d = jnp.where(signed >= 0, e, 1.0) * inv
            d = jnp.where(same, -d, d)
            PM[pl.ds(rg, 16), j : j + HALF] = (d * jnp.concatenate([scale] * 3, axis=1)).astype(BF16)
            for n, v in enumerate((term, d * dot, d)):
                for q in range(3):
                    w = v[:, 128 * q : 128 * q + 128]
                    sums[n] = sums[n] + (w[:8] + w[8:])
            return tuple(sums)

        zero = jnp.zeros((8, 128), F32)
        sums = lax.fori_loop(0, 12, chunk, (zero, zero, zero))
        for n in range(3):
            acc[8 * n : 8 * n + 8, :] += sums[n]

    def image_grads(g):
        base = order[g] * (4 * ROWS)
        GI[rows_at(base, 4 * ROWS), :] = jnp.dot(PM[rows_at(base, 4 * ROWS), :], T[...], preferred_element_type=F32)

    def send_code(value, k, i, device, sem=None):
        encode(value, img_s.at[3 * k + i])
        return send(img_s.at[3 * k + i], img_r.at[3 * k + i], device, sem)

    def got(k, i):
        return decode(img_r.at[3 * k + i], SUB)

    def part(row, i):
        return GI.at[rows_at(row + i * SUB, SUB, SUB), :]

    messages, second = {}, {}

    def first_sends(g):
        base = order[g] * (4 * ROWS)
        for n, place in enumerate((2, 1, 3)):
            messages[3 * g + n] = [
                send_code(part(base + place * ROWS, i)[...], 3 * g + n, i, at_a(place)) for i in range(3)]

    def first_sum(g, i):
        value = part(order[g] * (4 * ROWS), i)[...]
        for k in range(3 * g, 3 * g + 3):
            messages[k][i].wait_recv()
            value = value + got(k, i)
        return value

    def close(g):
        k = 11 + order[g]
        if g == 0:
            second["sem"] = count[0]
            count[0] += 9
        second[g] = [
            send_code(first_sum(g, i), k, i, at_b(order[g]), second["sem"] + 3 * (order[g] - 1) + i) for i in range(3)]

    drained = [0, len(sent)]

    def drain():
        for copy in sent[drained[0] : drained[1]]:
            copy.wait_send()
        drained[:] = drained[1], len(sent)

    cores = {}

    def text_grads(g):
        n = len(GROUPS[g]) * ROWS
        base = text_row(GROUPS[g][0], 0)
        GT[pl.ds(base, 2 * n), :] = lax.dot_general(PM[:, base : base + 2 * n], I[...], (((0,), (0,)), ((), ())),
                                                    preferred_element_type=F32)
        for rel in GROUPS[g]:
            cores[rel] = send(GT.at[pl.ds(text_row(rel, 1), ROWS)], RT.at[pl.ds(rel * ROWS, ROWS)], at_core)

    def text_sum(rel, i):
        row = text_row(rel, 0) + i * SUB
        return GT[row : row + SUB, :] + RT[rel * ROWS + i * SUB : rel * ROWS + (i + 1) * SUB, :]

    zs = {}

    def z_send(k, rel, distance, incoming=()):
        zs[k] = []
        cores[rel].wait_recv()
        for i in range(3):
            value = text_sum(rel, i)
            for j in incoming:
                zs[j][i].wait_recv()
                value = value + decode(txt_r.at[3 * j + i], SUB)
            encode(value, txt_s.at[3 * k + i])
            zs[k].append(send(txt_s.at[3 * k + i], txt_r.at[3 * k + i], at_z(distance)))

    for g in range(4):
        pair(g, 0)
    text_grads(0)
    for g in range(4):
        pair(g, HALF)
        image_grads(g)
        first_sends(g)
        if g == 0:
            z_send(0, 4, 2)
            z_send(1, 3, 1)
            z_send(2, 5, 7)
            drain()
        elif g == 2:
            close(0)
    text_grads(1)
    sc_s[0] = acc[...]
    over_core = send(sc_s.at[0], sc_c, at_core)
    close(1)
    z_send(3, 6, 7, (2,))
    z_send(4, 2, 1, (1, 0))
    over_core.wait_recv()
    sc_s[1] = sc_s[0] + sc_c[...]
    sc_x[x] = sc_s[1]
    over_x = [send(sc_s.at[1], sc_x.at[x], at_x(d)) for d in (1, 2, 3)]
    close(2)
    text_grads(2)
    wait(over_x)
    sc_s[2] = (sc_x[0] + sc_x[1]) + (sc_x[2] + sc_x[3])
    sc_y[y] = sc_s[2]
    over_y = [send(sc_s.at[2], sc_y.at[y], at_y(d)) for d in (1, 2, 3)]
    drain()
    z_send(5, 7, 7, (3,))
    z_send(6, 1, 1, (4,))
    twin, side, across = [], [], []
    for i in range(3):
        value = first_sum(3, i)
        for g in range(3):
            second[g][i].wait_recv()
        for k in (12, 13, 14):
            value = value + got(k, i)
        twin.append(send_code(value, 15, i, at_y(dyt)))
        side.append(send(img_s.at[45 + i], img_r.at[48 + i], at_core))

    def image_out(row, i):
        return gimg_o.at[rows_at(row + i * SUB, SUB, SUB), :]

    for i in range(3):
        image_out(own_row, i)[...] = decode(img_s.at[45 + i], SUB)
    drain()
    wait(over_y)
    sc_s[3] = (sc_y[0] + sc_y[1]) + (sc_y[2] + sc_y[3])
    sc_z[z] = sc_s[3]
    over_z = [send(sc_s.at[3], sc_z.at[z], at_z(d)) for d in range(1, 8)]
    for i in range(3):
        side[i].wait_recv()
        image_out((lo * 2 + 1 - c) * ROWS, i)[...] = got(16, i)
    for i in range(3):
        twin[i].wait_recv()
        across.append(send(img_r.at[45 + i], img_r.at[51 + i], at_core))
        image_out(twin_row, i)[...] = got(15, i)
    for i in range(3):
        across[i].wait_recv()
        image_out(((1 - lo) * 2 + 1 - c) * ROWS, i)[...] = got(17, i)
    for i in range(3):
        if i == 0:
            cores[0].wait_recv()
        zs[5][i].wait_recv()
        zs[6][i].wait_recv()
        gtxt_o[i * SUB : i * SUB + SUB, :] = (
            text_sum(0, i) + decode(txt_r.at[15 + i], SUB) + decode(txt_r.at[18 + i], SUB))
    wait(over_z)
    total = sc_z[0]
    for i in range(1, 8):
        total = total + sc_z[i]
    pairs = 1.0 / (256.0 * ROWS * 256.0 * ROWS)
    loss_o[0] = -jnp.sum(total[0:8]) * pairs
    temp_o[0] = jnp.sum(total[8:16]) * pairs
    bias_o[0] = jnp.sum(total[16:24]) * pairs
    drain()
    drain()


def local(images, texts, log_temp, bias):
    sems = 200
    vmem = pl.BlockSpec(memory_space=pltpu.VMEM)
    smem = pl.BlockSpec(memory_space=pltpu.SMEM)
    hbm = pl.BlockSpec(memory_space=pltpu.HBM)
    scalar = jax.ShapeDtypeStruct((1,), F32)
    V = pltpu.VMEM
    return pl.pallas_call(
        kernel,
        out_shape=(scalar, jax.ShapeDtypeStruct((4 * ROWS, D), F32), jax.ShapeDtypeStruct((ROWS, D), F32), scalar, scalar),
        in_specs=[hbm, hbm, smem, smem],
        out_specs=(smem, vmem, vmem, smem, smem),
        scratch_shapes=[
            V((SIDE, D), BF16), V((SIDE, D), BF16), V((SIDE, SIDE), BF16), V((4 * ROWS, HALF), F32),
            V((SIDE, D), F32), V((SIDE, D), F32), V((SIDE // 2, D), F32),
            V((SIDE, 128), jnp.int32), V((8, SIDE), jnp.int32),
            V((48, 10, 16, 128), BF16), V((54, 10, 16, 128), BF16), V((21, 10, 16, 128), BF16), V((21, 10, 16, 128), BF16),
            V((4, 24, 128), F32), V((4, 24, 128), F32), V((4, 24, 128), F32), V((8, 24, 128), F32),
            V((24, 128), F32), V((24, 128), F32),
            pltpu.SemaphoreType.DMA((sems,)), pltpu.SemaphoreType.DMA((sems,)), pltpu.SemaphoreType.DMA((3,)),
        ],
        compiler_params=pltpu.CompilerParams(collective_id=0, has_side_effects=True, vmem_limit_bytes=48 << 20),
        name="pairs",
    )(images, texts, log_temp, bias)


def solution(mesh):
    return jax.shard_map(
        local,
        mesh=mesh,
        in_specs=(P("grp", None), P(("blk", "grp"), None), P(), P()),
        out_specs=(P(), P("grp", None), P(("blk", "grp"), None), P(), P()),
        check_vma=False,
    )
```

time: 1080 us -> 71.3 us (0.07)
  waiting for transfers between devices: 953 us -> 0 us
  blocking collectives: 78.5 us -> 0 us
  Pallas kernels: 0 us -> 59.3 us
  matrix products: 19 us -> 0 us
  between operations: 20.4 us -> 7.18 us
    reduce_scatter x1 -> x0, waiting for transfers between devices: 808 us -> none  [local(): lax.psum_scatter(partial_value, 'grp', scatter_dimension=0, tiled=True)]
    all_gather x1 -> x0, waiting for transfers between devices: 144 us -> none  [local(): quarter_txt = lax.all_gather(texts, 'grp', axis=0, tiled=True)]
    psum x1 -> x0, blocking collectives: 78.5 us -> none  [local(): lax.psum((loss_sum, temp_sum, bias_sum), ('blk', 'grp'))]
    pallas_call x0 -> x1, Pallas kernels: none -> 59.3 us  [local(): pl.pallas_call(kernel, out_shape=(scalar, jax.ShapeDtypeStruct((4 * ROWS,...]
    dot_general x3 -> x0, matrix products: 19 us -> none  [the longest x1 8.06 us: local(): partial_value = jnp.dot(coef.T, images, preferred_element_type=jnp.float32)]
  transfers between devices with their start and end apart: 3 -> 0, of which waited for: 2 -> 0; matrix products, arithmetic and copies ran while one was open for 1% -> 0% of each run, Pallas kernels for 0% -> 0%
where the time goes in v2:
time: 71.3 us; the launch traced here: 70 us
  Pallas kernels  59.3 us (83%)
  between operations  7.18 us (10%)
  local copies, waits for them, and re-layouts  3.5 us (5%)
    pallas_call x1, Pallas kernels, local(): pl.pallas_call(kernel, out_shape=(scalar, jax.ShapeDtypeStruct((4 * ROWS,...  59.3 us
    unnamed x6, local copies, waits for them, and re-layouts  3.5 us

profile of v2, /device:TPU:1, one launch (start us, length us, event | category | flops | bytes accessed | tf_op | source)
XLA Modules:
  0.0 70.0 jit_solution(1738540139435083669)
XLA Ops:
  1.9 0.0 copy-start
  1.9 1.0 %copy-done = bf16[192,1152]{1,0:T(8,128)(2,1)S(1)} copy-done((bf16[192,1152]{1,0:T(8,128)(2,1)S(1)}, bf16[192,1152]{1,0:T(8,128)(2,1)}, u32[]{:S(2)}) %copy-start) | copy-done | bytes 442392
  2.9 0.0 copy-start.1
  2.9 0.9 %copy-done.1 = bf16[48,1152]{1,0:T(8,128)(2,1)S(1)} copy-done((bf16[48,1152]{1,0:T(8,128)(2,1)S(1)}, bf16[48,1152]{1,0:T(8,128)(2,1)}, u32[]{:S(2)}) %copy-start.1) | copy-done | bytes 110616
  3.8 59.3 %pairs.1 = (f32[1]{0:T(128)}, f32[192,1152]{1,0:T(8,128)S(1)}, f32[48,1152]{1,0:T(8,128)S(1)}, f32[1]{0:T(128)}, f32[1]{0:T(128)}) custom-call(bf16[192,1152]{1,0:T(8,128)(2,1)S(1)} %copy-done, bf16[48,1152]{1,0:T(8,128)(2,1)S(1)} %copy-done.1, f32[1]{0:T(128)S(6)} %copy.14.lt, f32[1]{0:T(128)S(6)} %copy.15.bs), custom_call_target="tpu_custom_call" | custom-call | tf_op jit(solution)/shard_map/pairs/pallas_call | solution.py:421
  63.8 0.9 %copy.17 = f32[192,1152]{1,0:T(8,128)} copy(f32[192,1152]{1,0:T(8,128)S(1)} %get-tuple-element.11) | data formatting | bytes 1769472
  64.7 0.7 copy.18
Async XLA Ops:
  1.9 1.0 %copy-start = (bf16[192,1152]{1,0:T(8,128)(2,1)S(1)}, bf16[192,1152]{1,0:T(8,128)(2,1)}, u32[]{:S(2)}) copy-start(bf16[192,1152]{1,0:T(8,128)(2,1)} %img.1) | copy-start | bytes 1327108
  2.9 0.9 %copy-start.1 = (bf16[48,1152]{1,0:T(8,128)(2,1)S(1)}, bf16[48,1152]{1,0:T(8,128)(2,1)}, u32[]{:S(2)}) copy-start(bf16[48,1152]{1,0:T(8,128)(2,1)} %txt.1) | copy-start | bytes 331780

commit v3 on v2

--- a/solution.py
+++ b/solution.py
@@ -217,12 +217,6 @@
     for i in range(3):
         t4[i].wait_recv()
         t_c.append([hop(T, text_row(4, 0), T, text_row(4, 1), i, at_core)])
-    for copies in t_c:
-        wait(copies)
-    for copy in mine:
-        copy.wait()
-    for copies in (xpf, xmf, w0, w1, w2, v1, v2):
-        wait(copies)
 
     g1 = (1 + 2 * lo) * (1 - c) + c
     order = (2, g1, 4 - g1, 0)
@@ -329,39 +323,53 @@
             encode(value, txt_s.at[3 * k + i])
             zs[k].append(send(txt_s.at[3 * k + i], txt_r.at[3 * k + i], at_z(distance)))
 
-    for g in range(4):
+    for copies in t_c[:5]:
+        wait(copies)
+    for copy in mine:
+        copy.wait()
+    for copies in (xpf, xmf, w0):
+        wait(copies)
+    pair(3, HALF)
+    for copies in t_c[5:]:
+        wait(copies)
+    for copies in (w1, w2, v1, v2):
+        wait(copies)
+    for g in (0, 1):
         pair(g, 0)
-    text_grads(0)
-    for g in range(4):
         pair(g, HALF)
         image_grads(g)
         first_sends(g)
-        if g == 0:
-            z_send(0, 4, 2)
-            z_send(1, 3, 1)
-            z_send(2, 5, 7)
-            drain()
-        elif g == 2:
-            close(0)
+    pair(2, 0)
+    pair(3, 0)
+    text_grads(0)
+    pair(2, HALF)
+    sc_s[0] = acc[...]
+    sc_x[x] = sc_s[0]
+    over_x = [send(sc_s.at[0], sc_x.at[x], at_x(d)) for d in (1, 2, 3)]
+    image_grads(2)
+    first_sends(2)
+    z_send(0, 4, 2)
+    z_send(1, 3, 1)
+    z_send(2, 5, 7)
+    image_grads(3)
+    first_sends(3)
+    close(0)
     text_grads(1)
-    sc_s[0] = acc[...]
-    over_core = send(sc_s.at[0], sc_c, at_core)
+    wait(over_x)
+    sc_s[1] = (sc_x[0] + sc_x[1]) + (sc_x[2] + sc_x[3])
+    sc_y[y] = sc_s[1]
+    over_y = [send(sc_s.at[1], sc_y.at[y], at_y(d)) for d in (1, 2, 3)]
+    drain()
     close(1)
     z_send(3, 6, 7, (2,))
     z_send(4, 2, 1, (1, 0))
-    over_core.wait_recv()
-    sc_s[1] = sc_s[0] + sc_c[...]
-    sc_x[x] = sc_s[1]
-    over_x = [send(sc_s.at[1], sc_x.at[x], at_x(d)) for d in (1, 2, 3)]
     close(2)
+    wait(over_y)
+    sc_s[2] = (sc_y[0] + sc_y[1]) + (sc_y[2] + sc_y[3])
+    sc_z[z] = sc_s[2]
+    over_z = [send(sc_s.at[2], sc_z.at[z], at_z(d)) for d in range(1, 8)]
     text_grads(2)
-    wait(over_x)
-    sc_s[2] = (sc_x[0] + sc_x[1]) + (sc_x[2] + sc_x[3])
-    sc_y[y] = sc_s[2]
-    over_y = [send(sc_s.at[2], sc_y.at[y], at_y(d)) for d in (1, 2, 3)]
-    drain()
-    z_send(5, 7, 7, (3,))
-    z_send(6, 1, 1, (4,))
+    drain()
     twin, side, across = [], [], []
     for i in range(3):
         value = first_sum(3, i)
@@ -371,27 +379,35 @@
             value = value + got(k, i)
         twin.append(send_code(value, 15, i, at_y(dyt)))
         side.append(send(img_s.at[45 + i], img_r.at[48 + i], at_core))
+    z_send(5, 7, 7, (3,))
+    z_send(6, 1, 1, (4,))
+
+    wait(over_z)
+    total = sc_z[0]
+    for i in range(1, 8):
+        total = total + sc_z[i]
+    sc_s[3] = total
+    over_core = send(sc_s.at[3], sc_c, at_core)
 
     def image_out(row, i):
         return gimg_o.at[rows_at(row + i * SUB, SUB, SUB), :]
 
+    drain()
     for i in range(3):
         image_out(own_row, i)[...] = decode(img_s.at[45 + i], SUB)
-    drain()
-    wait(over_y)
-    sc_s[3] = (sc_y[0] + sc_y[1]) + (sc_y[2] + sc_y[3])
-    sc_z[z] = sc_s[3]
-    over_z = [send(sc_s.at[3], sc_z.at[z], at_z(d)) for d in range(1, 8)]
     for i in range(3):
         side[i].wait_recv()
         image_out((lo * 2 + 1 - c) * ROWS, i)[...] = got(16, i)
+    over_core.wait_recv()
+    total = sc_s[3] + sc_c[...]
+    pairs = 1.0 / (256.0 * ROWS * 256.0 * ROWS)
+    loss_o[0] = -jnp.sum(total[0:8]) * pairs
+    temp_o[0] = jnp.sum(total[8:16]) * pairs
+    bias_o[0] = jnp.sum(total[16:24]) * pairs
     for i in range(3):
         twin[i].wait_recv()
         across.append(send(img_r.at[45 + i], img_r.at[51 + i], at_core))
         image_out(twin_row, i)[...] = got(15, i)
-    for i in range(3):
-        across[i].wait_recv()
-        image_out(((1 - lo) * 2 + 1 - c) * ROWS, i)[...] = got(17, i)
     for i in range(3):
         if i == 0:
             cores[0].wait_recv()
@@ -399,14 +415,10 @@
         zs[6][i].wait_recv()
         gtxt_o[i * SUB : i * SUB + SUB, :] = (
             text_sum(0, i) + decode(txt_r.at[15 + i], SUB) + decode(txt_r.at[18 + i], SUB))
-    wait(over_z)
-    total = sc_z[0]
-    for i in range(1, 8):
-        total = total + sc_z[i]
-    pairs = 1.0 / (256.0 * ROWS * 256.0 * ROWS)
-    loss_o[0] = -jnp.sum(total[0:8]) * pairs
-    temp_o[0] = jnp.sum(total[8:16]) * pairs
-    bias_o[0] = jnp.sum(total[16:24]) * pairs
+    drain()
+    for i in range(3):
+        across[i].wait_recv()
+        image_out(((1 - lo) * 2 + 1 - c) * ROWS, i)[...] = got(17, i)
     drain()
     drain()
 

time: 71.3 us -> 69.1 us (0.969); the launches traced: 70 us -> 68.8 us
  Pallas kernels: 59.3 us -> 58.2 us
    pallas_call x1, Pallas kernels: 59.3 us -> 58.2 us  [local(): pl.pallas_call(kernel, out_shape=(scalar, jax.ShapeDtypeStruct((4 * ROWS,...]
where the time goes in v3:
time: 69.1 us; the launch traced here: 68.8 us
  Pallas kernels  58.2 us (84%)
  between operations  7.18 us (10%)
  local copies, waits for them, and re-layouts  3.5 us (5%)
    pallas_call x1, Pallas kernels, local(): pl.pallas_call(kernel, out_shape=(scalar, jax.ShapeDtypeStruct((4 * ROWS,...  58.2 us
    unnamed x6, local copies, waits for them, and re-layouts  3.5 us

profile of v3, /device:TPU:1, one launch (start us, length us, event | category | flops | bytes accessed | tf_op | source)
XLA Modules:
  0.0 68.8 jit_solution(11052773669918050865)
XLA Ops:
  1.9 0.0 copy-start
  1.9 1.0 %copy-done = bf16[192,1152]{1,0:T(8,128)(2,1)S(1)} copy-done((bf16[192,1152]{1,0:T(8,128)(2,1)S(1)}, bf16[192,1152]{1,0:T(8,128)(2,1)}, u32[]{:S(2)}) %copy-start) | copy-done | bytes 442392
  2.9 0.0 copy-start.1
  2.9 0.9 %copy-done.1 = bf16[48,1152]{1,0:T(8,128)(2,1)S(1)} copy-done((bf16[48,1152]{1,0:T(8,128)(2,1)S(1)}, bf16[48,1152]{1,0:T(8,128)(2,1)}, u32[]{:S(2)}) %copy-start.1) | copy-done | bytes 110616
  3.8 58.2 %pairs.1 = (f32[1]{0:T(128)}, f32[192,1152]{1,0:T(8,128)S(1)}, f32[48,1152]{1,0:T(8,128)S(1)}, f32[1]{0:T(128)}, f32[1]{0:T(128)}) custom-call(bf16[192,1152]{1,0:T(8,128)(2,1)S(1)} %copy-done, bf16[48,1152]{1,0:T(8,128)(2,1)S(1)} %copy-done.1, f32[1]{0:T(128)S(6)} %copy.14.lt, f32[1]{0:T(128)S(6)} %copy.15.bs), custom_call_target="tpu_custom_call" | custom-call | tf_op jit(solution)/shard_map/pairs/pallas_call | solution.py:433
  62.6 0.9 %copy.17 = f32[192,1152]{1,0:T(8,128)} copy(f32[192,1152]{1,0:T(8,128)S(1)} %get-tuple-element.11) | data formatting | bytes 1769472
  63.5 0.7 copy.18
Async XLA Ops:
  1.9 1.0 %copy-start = (bf16[192,1152]{1,0:T(8,128)(2,1)S(1)}, bf16[192,1152]{1,0:T(8,128)(2,1)}, u32[]{:S(2)}) copy-start(bf16[192,1152]{1,0:T(8,128)(2,1)} %img.1) | copy-start | bytes 1327108
  2.9 0.9 %copy-start.1 = (bf16[48,1152]{1,0:T(8,128)(2,1)S(1)}, bf16[48,1152]{1,0:T(8,128)(2,1)}, u32[]{:S(2)}) copy-start(bf16[48,1152]{1,0:T(8,128)(2,1)} %txt.1) | copy-start | bytes 331780

commit v4 on v3

--- a/solution.py
+++ b/solution.py
@@ -256,12 +256,15 @@
         base = order[g] * (4 * ROWS)
         GI[rows_at(base, 4 * ROWS), :] = jnp.dot(PM[rows_at(base, 4 * ROWS), :], T[...], preferred_element_type=F32)
 
+    def box(ref, n, tiles=10):
+        return ref.at[pl.ds(n * 10, tiles)]
+
     def send_code(value, k, i, device, sem=None):
-        encode(value, img_s.at[3 * k + i])
-        return send(img_s.at[3 * k + i], img_r.at[3 * k + i], device, sem)
+        encode(value, box(img_s, 3 * k + i))
+        return send(box(img_s, 3 * k + i), box(img_r, 3 * k + i), device, sem)
 
     def got(k, i):
-        return decode(img_r.at[3 * k + i], SUB)
+        return decode(box(img_r, 3 * k + i), SUB)
 
     def part(row, i):
         return GI.at[rows_at(row + i * SUB, SUB, SUB), :]
@@ -271,7 +274,12 @@
     def first_sends(g):
         base = order[g] * (4 * ROWS)
         for n, place in enumerate((2, 1, 3)):
-            messages[3 * g + n] = [
+            k = 3 * g + n
+            if g < 3:
+                encode(GI[rows_at(base + place * ROWS, ROWS), :], box(img_s, 3 * k, 28))
+                messages[k] = send(box(img_s, 3 * k, 28), box(img_r, 3 * k, 28), at_a(place))
+                continue
+            messages[k] = [
                 send_code(part(base + place * ROWS, i)[...], 3 * g + n, i, at_a(place)) for i in range(3)]
 
     def first_sum(g, i):
@@ -286,8 +294,12 @@
         if g == 0:
             second["sem"] = count[0]
             count[0] += 9
+        total = GI[rows_at(order[g] * (4 * ROWS), ROWS), :]
+        for n in range(3 * g, 3 * g + 3):
+            messages[n].wait_recv()
+            total = total + decode(box(img_r, 3 * n, 28), ROWS)
         second[g] = [
-            send_code(first_sum(g, i), k, i, at_b(order[g]), second["sem"] + 3 * (order[g] - 1) + i) for i in range(3)]
+            send_code(total[i * SUB : (i + 1) * SUB], k, i, at_b(order[g]), second["sem"] + 3 * (order[g] - 1) + i) for i in range(3)]
 
     drained = [0, len(sent)]
 
@@ -378,7 +390,7 @@
         for k in (12, 13, 14):
             value = value + got(k, i)
         twin.append(send_code(value, 15, i, at_y(dyt)))
-        side.append(send(img_s.at[45 + i], img_r.at[48 + i], at_core))
+        side.append(send(box(img_s, 45 + i), box(img_r, 48 + i), at_core))
     z_send(5, 7, 7, (3,))
     z_send(6, 1, 1, (4,))
 
@@ -394,7 +406,7 @@
 
     drain()
     for i in range(3):
-        image_out(own_row, i)[...] = decode(img_s.at[45 + i], SUB)
+        image_out(own_row, i)[...] = decode(box(img_s, 45 + i), SUB)
     for i in range(3):
         side[i].wait_recv()
         image_out((lo * 2 + 1 - c) * ROWS, i)[...] = got(16, i)
@@ -406,7 +418,7 @@
     bias_o[0] = jnp.sum(total[16:24]) * pairs
     for i in range(3):
         twin[i].wait_recv()
-        across.append(send(img_r.at[45 + i], img_r.at[51 + i], at_core))
+        across.append(send(box(img_r, 45 + i), box(img_r, 51 + i), at_core))
         image_out(twin_row, i)[...] = got(15, i)
     for i in range(3):
         if i == 0:
@@ -439,7 +451,7 @@
             V((SIDE, D), BF16), V((SIDE, D), BF16), V((SIDE, SIDE), BF16), V((4 * ROWS, HALF), F32),
             V((SIDE, D), F32), V((SIDE, D), F32), V((SIDE // 2, D), F32),
             V((SIDE, 128), jnp.int32), V((8, SIDE), jnp.int32),
-            V((48, 10, 16, 128), BF16), V((54, 10, 16, 128), BF16), V((21, 10, 16, 128), BF16), V((21, 10, 16, 128), BF16),
+            V((480, 16, 128), BF16), V((540, 16, 128), BF16), V((21, 10, 16, 128), BF16), V((21, 10, 16, 128), BF16),
             V((4, 24, 128), F32), V((4, 24, 128), F32), V((4, 24, 128), F32), V((8, 24, 128), F32),
             V((24, 128), F32), V((24, 128), F32),
             pltpu.SemaphoreType.DMA((sems,)), pltpu.SemaphoreType.DMA((sems,)), pltpu.SemaphoreType.DMA((3,)),

time: 69.1 us -> 68.7 us (level)
  no operation moved by 1% of the time
where the time goes in v4:
time: 68.7 us; the launch traced here: 68.5 us
  Pallas kernels  57.8 us (84%)
  between operations  7.18 us (10%)
  local copies, waits for them, and re-layouts  3.5 us (5%)
    pallas_call x1, Pallas kernels, local(): pl.pallas_call(kernel, out_shape=(scalar, jax.ShapeDtypeStruct((4 * ROWS,...  57.8 us
    unnamed x6, local copies, waits for them, and re-layouts  3.5 us

profile of v4, /device:TPU:1, one launch (start us, length us, event | category | flops | bytes accessed | tf_op | source)
XLA Modules:
  0.0 68.5 jit_solution(4993734818360069727)
XLA Ops:
  1.9 0.0 copy-start
  1.9 1.0 %copy-done = bf16[192,1152]{1,0:T(8,128)(2,1)S(1)} copy-done((bf16[192,1152]{1,0:T(8,128)(2,1)S(1)}, bf16[192,1152]{1,0:T(8,128)(2,1)}, u32[]{:S(2)}) %copy-start) | copy-done | bytes 442392
  2.9 0.0 copy-start.1
  2.9 0.9 %copy-done.1 = bf16[48,1152]{1,0:T(8,128)(2,1)S(1)} copy-done((bf16[48,1152]{1,0:T(8,128)(2,1)S(1)}, bf16[48,1152]{1,0:T(8,128)(2,1)}, u32[]{:S(2)}) %copy-start.1) | copy-done | bytes 110616
  3.8 57.8 %pairs.1 = (f32[1]{0:T(128)}, f32[192,1152]{1,0:T(8,128)S(1)}, f32[48,1152]{1,0:T(8,128)S(1)}, f32[1]{0:T(128)}, f32[1]{0:T(128)}) custom-call(bf16[192,1152]{1,0:T(8,128)(2,1)S(1)} %copy-done, bf16[48,1152]{1,0:T(8,128)(2,1)S(1)} %copy-done.1, f32[1]{0:T(128)S(6)} %copy.14.lt, f32[1]{0:T(128)S(6)} %copy.15.bs), custom_call_target="tpu_custom_call" | custom-call | tf_op jit(solution)/shard_map/pairs/pallas_call | solution.py:445
  62.2 0.9 %copy.17 = f32[192,1152]{1,0:T(8,128)} copy(f32[192,1152]{1,0:T(8,128)S(1)} %get-tuple-element.11) | data formatting | bytes 1769472
  63.2 0.7 %copy.18 = f32[48,1152]{1,0:T(8,128)} copy(f32[48,1152]{1,0:T(8,128)S(1)} %get-tuple-element.12) | data formatting | bytes 442368
Async XLA Ops:
  1.9 1.0 %copy-start = (bf16[192,1152]{1,0:T(8,128)(2,1)S(1)}, bf16[192,1152]{1,0:T(8,128)(2,1)}, u32[]{:S(2)}) copy-start(bf16[192,1152]{1,0:T(8,128)(2,1)} %img.1) | copy-start | bytes 1327108
  2.9 0.9 %copy-start.1 = (bf16[48,1152]{1,0:T(8,128)(2,1)S(1)}, bf16[48,1152]{1,0:T(8,128)(2,1)}, u32[]{:S(2)}) copy-start(bf16[48,1152]{1,0:T(8,128)(2,1)} %txt.1) | copy-start | bytes 331780
